TPU v7x, 32 devices: a whole 2x2x4 slice. The times are simulated.
32 devices in a mesh: groups: 2 (over y), blk: 4 (over x, core), rep: 4 (over z).
Axes of the slice: x: 2, y: 2, z: 4, core: 2. Of those that a mesh axis runs over, the one named last changes fastest.
Arguments:
- features: bfloat16 [8192, 256], P(('groups', 'blk')), parts along dimension 0, may hold values from -6 to 6
- weight: bfloat16 [256, 256], replicated, may hold values from -0.375 to 0.375
- cotangent: bfloat16 [8192, 256], P(('groups', 'blk', 'rep')), parts along dimension 0, may hold values from -6 to 6
- tiles: bfloat16 [8, 4, 4, 2, 256, 256], P(('groups', 'blk'), 'rep'), parts along dimension 0, may hold values from -0.1875 to 0.1875
- tile_rows: int32 [8, 4, 4, 2], P(('groups', 'blk'), 'rep'), parts along dimension 0, may hold values from 0 to 3, as said below
- tile_cols: int32 [8, 4, 4, 2], P(('groups', 'blk'), 'rep'), parts along dimension 0, may hold values from 0 to 3
- tile_count: int32 [8, 4, 4], P(('groups', 'blk'), 'rep'), parts along dimension 0, may hold values from 0 to 2, as said below
Outputs:
- output: bfloat16 [8192, 256], P(('groups', 'blk', 'rep')), parts along dimension 0
- feature_grad: bfloat16 [8192, 256], P(('groups', 'blk', 'rep')), parts along dimension 0
- weight_grad: float32 [512, 256], P('groups'), parts along dimension 0
There are 2 independent parts, one for each index of `groups`. A program takes and returns all parts, laid end to end along the dimension named above; an argument that names none is the same for every part. Nothing has to cross between parts.
Inputs may be any that keep to these rules, and one draw needn't show every extreme that they name: `tile_count`: an owner reaches its own panels and those of its two neighbours along the loop from every device along rep, and uses all 2 slots on its own panels; any other owner is reached by all devices along rep or by none, and for every distance along the loop some owner reaches the owner that far away. `tile_rows`: for one row owner and one source owner, the slots of all devices along rep name distinct (row panel, column panel) pairs.
All inputs are finite; a program needn't handle non-finite values.
Results may differ from a plain program's by a relative error of at most 0.0065.
Values may be sent and summed in bfloat16 or wider, within the bound.
A program may use at most 64 MiB of HBM per device.

v0:
```python
import jax
import jax.numpy as jnp
from jax import lax
from jax.sharding import PartitionSpec as P


def from_behind(value, axis, steps):
    count = lax.axis_size(axis)
    pairs = [(source, (source + steps) % count) for source in range(count)]
    return lax.ppermute(value, axis, pairs)


def activation(values):
    return jax.nn.gelu(values, approximate=True)


def on_device(features, weight, cotangent, tiles, tile_rows, tile_cols, tile_count):
    tile_mats = tiles[0, 0]
    row_ids = tile_rows[0, 0]
    col_ids = tile_cols[0, 0]
    filled = tile_count[0, 0]
    cycle_size = lax.axis_size("blk")
    myself = lax.axis_index("blk")
    hidden = features.shape[1]
    tile_size = tile_mats.shape[-1]
    panels = features.shape[0] // tile_size
    slot_ids = jnp.arange(tile_mats.shape[1], dtype=jnp.int32)

    def source_parts(source):
        tile_blocks = lax.dynamic_index_in_dim(tile_mats, source, 0, keepdims=False)
        rows_here = lax.dynamic_index_in_dim(row_ids, source, 0, keepdims=False)
        cols_here = lax.dynamic_index_in_dim(col_ids, source, 0, keepdims=False)
        limit = lax.dynamic_index_in_dim(filled, source, 0, keepdims=False)
        active = (slot_ids < limit).astype(jnp.float32)[:, None, None]
        return (tile_blocks, rows_here, cols_here, active)

    def add_forward(source, held_block, partial_value):
        tile_blocks, rows_here, cols_here, active = source_parts(source)
        chosen = held_block.reshape(panels, tile_size, hidden)[cols_here]
        product = jnp.einsum(
            "sij,sjd->sid", tile_blocks, chosen, preferred_element_type=jnp.float32
        )
        return partial_value.at[rows_here].add(product * active)

    initial = add_forward(myself, features, jnp.zeros((panels, tile_size, hidden), jnp.float32))

    def forward_hop(hop_count, state_tuple):
        held_block, partial_value = state_tuple
        held_block = from_behind(held_block, "blk", 1)
        return (
            held_block,
            add_forward(jnp.mod(myself - hop_count, cycle_size), held_block, partial_value),
        )

    _, partial_value = lax.fori_loop(1, cycle_size, forward_hop, (features, initial))
    aggregated = lax.psum_scatter(
        partial_value.reshape(panels * tile_size, hidden), "rep", scatter_dimension=0, tiled=True
    ).astype(jnp.bfloat16)
    pre_act = jnp.dot(aggregated, weight, preferred_element_type=jnp.float32)
    output_vals, gelu_back = jax.vjp(activation, pre_act)
    output = output_vals.astype(jnp.bfloat16)
    pre_grad = gelu_back(cotangent.astype(jnp.float32))[0].astype(jnp.bfloat16)
    local_weight = jnp.dot(aggregated.T, pre_grad, preferred_element_type=jnp.float32)
    weight_grad = lax.psum(local_weight, ("blk", "rep"))
    agg_grad = jnp.dot(pre_grad, weight.T, preferred_element_type=jnp.float32).astype(jnp.bfloat16)
    grad_panels = lax.all_gather(agg_grad, "rep", axis=0, tiled=True).reshape(
        panels, tile_size, hidden
    )

    def add_backward(source, running):
        tile_blocks, rows_here, cols_here, active = source_parts(source)
        chosen = grad_panels[rows_here]
        product = jnp.einsum(
            "sij,sid->sjd", tile_blocks, chosen, preferred_element_type=jnp.float32
        )
        return running.at[cols_here].add(product * active)

    running = add_backward(
        jnp.mod(myself - 1, cycle_size), jnp.zeros((panels, tile_size, hidden), jnp.float32)
    )

    def back_hop(hop_count, running):
        running = from_behind(running, "blk", 1)
        return add_backward(jnp.mod(myself - 1 - hop_count, cycle_size), running)

    running = lax.fori_loop(1, cycle_size, back_hop, running)
    feature_grad = lax.psum_scatter(
        running.reshape(panels * tile_size, hidden), "rep", scatter_dimension=0, tiled=True
    ).astype(jnp.bfloat16)
    return (output, feature_grad, weight_grad)


def solution(mesh):
    in_specs = (
        P(("groups", "blk"), None),
        P(),
        P(("groups", "blk", "rep"), None),
        P(("groups", "blk"), "rep", None, None, None, None),
        P(("groups", "blk"), "rep", None, None),
        P(("groups", "blk"), "rep", None, None),
        P(("groups", "blk"), "rep", None),
    )
    out_specs = (
        P(("groups", "blk", "rep"), None),
        P(("groups", "blk", "rep"), None),
        P("groups", None),
    )
    return jax.shard_map(
        on_device, mesh=mesh, in_specs=in_specs, out_specs=out_specs, check_vma=False
    )
```

profile of v0, /device:TPU:1, one launch (start us, length us, event | category | flops | bytes accessed | tf_op | source)
XLA Modules:
  0.0 274.0 jit_solution(4301307892376939478)
XLA Ops:
  14.3 34.9 %while.34 = (s32[]{:T(128)}, bf16[1024,256]{1,0:T(8,128)(2,1)S(1)}, f32[4,256,256]{2,1,0:T(8,128)S(1)}, s32[]{:T(128)}, s32[4,2]{1,0:T(4,128)S(1)}, /*index=5*/b...) while((s32[]{:T(128)}, bf16[1024,256]{1,0:T(8,128)(2,1)S(1)}, ...), condition=%wide.region_3.4_spmd.clone, body=%wide.region_1.3_spmd.clone.sunk | while | flops 67372064 | bytes 6296624 | solution.py:55
  14.3 2.7 collective-permute-start
  18.8 4.3 %collective-permute-done = bf16[1024,256]{1,0:T(8,128)(2,1)S(1)} collective-permute-done((bf16[1024,256]{1,0:T(8,128)(2,1)S(1)}, bf16[1024,256]{1,0:T(8,128)(2,1)S(1)}, u32[]{:S(2)}, u32[]{:S(2)}) %collective-permute-start) | collective-permute-done | bytes 524320 | tf_op jit(solution)/shard_map/while/body/eval_jaxpr/ppermute | solution.py:10
  26.0 2.5 collective-permute-start
  30.3 4.3 %collective-permute-done = bf16[1024,256]{1,0:T(8,128)(2,1)S(1)} collective-permute-done((bf16[1024,256]{1,0:T(8,128)(2,1)S(1)}, bf16[1024,256]{1,0:T(8,128)(2,1)S(1)}, u32[]{:S(2)}, u32[]{:S(2)}) %collective-permute-start) | collective-permute-done | bytes 524320 | tf_op jit(solution)/shard_map/while/body/eval_jaxpr/ppermute | solution.py:10
  37.6 2.5 collective-permute-start
  41.9 4.3 %collective-permute-done = bf16[1024,256]{1,0:T(8,128)(2,1)S(1)} collective-permute-done((bf16[1024,256]{1,0:T(8,128)(2,1)S(1)}, bf16[1024,256]{1,0:T(8,128)(2,1)S(1)}, u32[]{:S(2)}, u32[]{:S(2)}) %collective-permute-start) | collective-permute-done | bytes 524320 | tf_op jit(solution)/shard_map/while/body/eval_jaxpr/ppermute | solution.py:10
  50.2 1.3 copy.10
  53.4 25.9 %reduce-scatter.3.cloned.1.call-done = f32[256,256]{1,0:T(8,128)} async-done(((f32[1024,256]{1,0:T(8,128)}), f32[256,256]{1,0:T(8,128)}) %reduce-scatter.3.cloned.1.call-update) | async-done | bytes 262160 | tf_op jit(solution)/shard_map/reduce_scatter | solution.py:56
  79.3 2.0 fusion.20
  81.9 12.1 %all_gather.3 = bf16[1024,256]{1,0:T(8,128)(2,1)S(1)} all-gather(bf16[256,256]{1,0:T(8,128)(2,1)S(1)} %convolution_convert_fusion), channel_id=1, replica_groups=mesh['groups'=2,'blk'=4,'rep'=4] {'rep'}, dimensions={0}, use_global_device_ids=true | all-gather | bytes 655360 | tf_op jit(solution)/shard_map/all_gather | solution.py:66
  95.7 50.6 %while.35 = (s32[]{:T(128)}, f32[4,256,256]{2,1,0:T(8,128)S(1)}, s32[]{:T(128)}, s32[4,2]{1,0:T(4,128)S(1)}, bf16[4,2,256,256]{2,3,1,0:T(8,128)(2,1)}, /*index=5...) while((s32[]{:T(128)}, f32[4,256,256]{2,1,0:T(8,128)S(1)}, ...), condition=%wide.region_8.9_spmd.clone, body=%wide.region_6.8_spmd.clone.sunk | while | flops 67372064 | bytes 9441872 | solution.py:86
  95.8 5.9 %collective-permute-start.1 = (f32[4,256,256]{2,1,0:T(8,128)S(1)}, f32[4,256,256]{2,1,0:T(8,128)S(1)}, u32[]{:S(2)}, u32[]{:S(2)}) collective-permute-start(f32[4,256,256]{2,1,0:T(8,128)S(1)} %get-tuple-element.703), channel_id=1, source_target_pairs={{0,4},{4,8},{8,12},{12,0},{1,5},{5,9},{9,13},{13,1},{2,6},{6,10},{... | collective-permute-start | bytes 3145736 | tf_op jit(solution)/shard_map/while/body/eval_jaxpr/ppermute | solution.py:10
  103.6 1.2 convolution_multiply_fusion.7
  104.8 8.6 %collective-permute-done.1 = f32[4,256,256]{2,1,0:T(8,128)S(1)} collective-permute-done((f32[4,256,256]{2,1,0:T(8,128)S(1)}, f32[4,256,256]{2,1,0:T(8,128)S(1)}, u32[]{:S(2)}, u32[]{:S(2)}) %collective-permute-start.1) | collective-permute-done | bytes 1048608 | tf_op jit(solution)/shard_map/while/body/eval_jaxpr/ppermute | solution.py:10
  114.9 2.5 collective-permute-start.1
  119.3 1.2 convolution_multiply_fusion.7
  120.5 8.6 %collective-permute-done.1 = f32[4,256,256]{2,1,0:T(8,128)S(1)} collective-permute-done((f32[4,256,256]{2,1,0:T(8,128)S(1)}, f32[4,256,256]{2,1,0:T(8,128)S(1)}, u32[]{:S(2)}, u32[]{:S(2)}) %collective-permute-start.1) | collective-permute-done | bytes 1048608 | tf_op jit(solution)/shard_map/while/body/eval_jaxpr/ppermute | solution.py:10
  130.7 2.5 collective-permute-start.1
  136.2 8.6 %collective-permute-done.1 = f32[4,256,256]{2,1,0:T(8,128)S(1)} collective-permute-done((f32[4,256,256]{2,1,0:T(8,128)S(1)}, f32[4,256,256]{2,1,0:T(8,128)S(1)}, u32[]{:S(2)}, u32[]{:S(2)}) %collective-permute-start.1) | collective-permute-done | bytes 1048608 | tf_op jit(solution)/shard_map/while/body/eval_jaxpr/ppermute | solution.py:10
  148.7 24.9 %reduce-scatter.5.cloned.1.call-done = f32[256,256]{1,0:T(8,128)} async-done(((f32[1024,256]{1,0:T(8,128)}), f32[256,256]{1,0:T(8,128)}) %reduce-scatter.5.cloned.1.call-update) | async-done | bytes 262160 | tf_op jit(solution)/shard_map/reduce_scatter | solution.py:87
  173.6 1.6 convert_element_type.67
  175.2 90.6 %all-reduce.2.cloned.1.call-done = f32[256,256]{1,0:T(8,128)} async-done(((f32[256,256]{1,0:T(8,128)}), f32[256,256]{1,0:T(8,128)}) %all-reduce.2.cloned.1.call-update) | async-done | bytes 262160 | tf_op jit(solution)/shard_map/psum | solution.py:64
  265.8 1.7 copy.40
  (125 shorter events, 40.1 us)
Async XLA Ops:
  7.2 72.1 %copy-start = (bf16[256,256]{1,0:T(8,128)(2,1)S(1)}, bf16[256,256]{1,0:T(8,128)(2,1)}, u32[]{:S(2)}) copy-start(bf16[256,256]{1,0:T(8,128)(2,1)} %param.12) | copy-start | bytes 393220
  7.2 5.9 %copy-start.2 = (bf16[1,1,4,2,256,256]{5,4,3,2,1,0:T(8,128)(2,1)S(1)}, bf16[1,1,4,2,256,256]{5,4,3,2,1,0:T(8,128)(2,1)}, u32[]{:S(2)}) copy-start(bf16[1,1,4,2,256,256]{5,4,3,2,1,0:T(8,128)(2,1)} %param.14) | copy-start | bytes 3145732
  7.2 72.1 %reduce-scatter.3.cloned.1.call-start = ((), (), s32[]{:S(2)}) async-start(), calls=%async_computation.2 | async-start | bytes 1310720 | tf_op jit(solution)/shard_map/reduce_scatter | solution.py:56
  10.3 0.7 copy-start.8
  11.0 0.7 copy-start.9
  14.3 8.8 %collective-permute-start = (bf16[1024,256]{1,0:T(8,128)(2,1)S(1)}, bf16[1024,256]{1,0:T(8,128)(2,1)S(1)}, u32[]{:S(2)}, u32[]{:S(2)}) collective-permute-start(bf16[1024,256]{1,0:T(8,128)(2,1)S(1)} %get-tuple-element.667), channel_id=1, source_target_pairs={{0,4},{4,8},{8,12},{12,0},{1,5},{5,9},{9,13},{13,1},{2,6},{6,10},{... | collective-permute-start | bytes 1572872 | tf_op jit(solution)/shard_map/while/body/eval_jaxpr/ppermute | solution.py:10
  25.3 0.7 copy-start.11
  26.0 8.6 %collective-permute-start = (bf16[1024,256]{1,0:T(8,128)(2,1)S(1)}, bf16[1024,256]{1,0:T(8,128)(2,1)S(1)}, u32[]{:S(2)}, u32[]{:S(2)}) collective-permute-start(bf16[1024,256]{1,0:T(8,128)(2,1)S(1)} %get-tuple-element.667), channel_id=1, source_target_pairs={{0,4},{4,8},{8,12},{12,0},{1,5},{5,9},{9,13},{13,1},{2,6},{6,10},{... | collective-permute-start | bytes 1572872 | tf_op jit(solution)/shard_map/while/body/eval_jaxpr/ppermute | solution.py:10
  36.9 0.7 copy-start.11
  37.6 8.6 %collective-permute-start = (bf16[1024,256]{1,0:T(8,128)(2,1)S(1)}, bf16[1024,256]{1,0:T(8,128)(2,1)S(1)}, u32[]{:S(2)}, u32[]{:S(2)}) collective-permute-start(bf16[1024,256]{1,0:T(8,128)(2,1)S(1)} %get-tuple-element.667), channel_id=1, source_target_pairs={{0,4},{4,8},{8,12},{12,0},{1,5},{5,9},{9,13},{13,1},{2,6},{6,10},{... | collective-permute-start | bytes 1572872 | tf_op jit(solution)/shard_map/while/body/eval_jaxpr/ppermute | solution.py:10
  49.1 1.0 copy-start.1
  50.2 123.4 %reduce-scatter.5.cloned.1.call-start = ((), (), s32[]{:S(2)}) async-start(), calls=%async_computation.3 | async-start | bytes 1310720 | tf_op jit(solution)/shard_map/reduce_scatter | solution.py:87
  50.2 29.0 %copy-start.16 = (bf16[256,256]{1,0:T(8,128)(2,1)S(1)}, bf16[256,256]{1,0:T(8,128)(2,1)}, u32[]{:S(2)}) copy-start(bf16[256,256]{1,0:T(8,128)(2,1)} %param.13) | copy-start | bytes 393220
  52.7 0.7 copy-start.14
  95.8 5.9 %copy-start.12 = (s32[4]{0:T(128)}, s32[4]{0:T(128)S(1)}, u32[]{:S(2)}) copy-start(s32[4]{0:T(128)S(1)} %get-tuple-element.721) | copy-start | bytes 52 | tf_op jit(solution)/shard_map/while
  95.8 17.7 %collective-permute-start.1 = (f32[4,256,256]{2,1,0:T(8,128)S(1)}, f32[4,256,256]{2,1,0:T(8,128)S(1)}, u32[]{:S(2)}, u32[]{:S(2)}) collective-permute-start(f32[4,256,256]{2,1,0:T(8,128)S(1)} %get-tuple-element.703), channel_id=1, source_target_pairs={{0,4},{4,8},{8,12},{12,0},{1,5},{5,9},{9,13},{13,1},{2,6},{6,10},{... | collective-permute-start | bytes 3145736 | tf_op jit(solution)/shard_map/while/body/eval_jaxpr/ppermute | solution.py:10
  114.9 2.5 copy-start.12
  114.9 14.2 %collective-permute-start.1 = (f32[4,256,256]{2,1,0:T(8,128)S(1)}, f32[4,256,256]{2,1,0:T(8,128)S(1)}, u32[]{:S(2)}, u32[]{:S(2)}) collective-permute-start(f32[4,256,256]{2,1,0:T(8,128)S(1)} %get-tuple-element.703), channel_id=1, source_target_pairs={{0,4},{4,8},{8,12},{12,0},{1,5},{5,9},{9,13},{13,1},{2,6},{6,10},{... | collective-permute-start | bytes 3145736 | tf_op jit(solution)/shard_map/while/body/eval_jaxpr/ppermute | solution.py:10
  130.7 2.5 copy-start.12
  130.7 14.2 %collective-permute-start.1 = (f32[4,256,256]{2,1,0:T(8,128)S(1)}, f32[4,256,256]{2,1,0:T(8,128)S(1)}, u32[]{:S(2)}, u32[]{:S(2)}) collective-permute-start(f32[4,256,256]{2,1,0:T(8,128)S(1)} %get-tuple-element.703), channel_id=1, source_target_pairs={{0,4},{4,8},{8,12},{12,0},{1,5},{5,9},{9,13},{13,1},{2,6},{6,10},{... | collective-permute-start | bytes 3145736 | tf_op jit(solution)/shard_map/while/body/eval_jaxpr/ppermute | solution.py:10
  146.4 1.0 copy-start.3
  146.4 1.0 copy-start.5
  146.4 1.3 copy-start.6
  147.4 118.4 %all-reduce.2.cloned.1.call-start = ((), (), s32[]{:S(2)}) async-start(), calls=%async_computation.4 | async-start | bytes 524288 | tf_op jit(solution)/shard_map/psum | solution.py:64
  (10 other events, 6.3 us)
Sparse Core Ops, SparseCore 0:
  50.3 28.9 reduce-scatter.2
  147.5 26.0 reduce-scatter.4
  177.5 88.2 all-reduce.1
where the time goes:
time: 275 us; the launch traced here: 274 us
  waiting for transfers between devices  180 us (65%)
  local copies, waits for them, and re-layouts  26.1 us (9%)
  starting transfers between devices  18.6 us (7%)
  other arithmetic  14.9 us (5%)
  between operations  13.9 us (5%)
  blocking collectives  12.1 us (4%)
  matrix products  7.84 us (3%)
    psum x1, waiting for transfers between devices, on_device(): weight_grad = lax.psum(local_weight, ('blk', 'rep'))  90.6 us
    ppermute x6, waiting for transfers between devices, from_behind(): return lax.ppermute(value, axis, pairs)  38.7 us
    reduce_scatter x1, waiting for transfers between devices, on_device(): lax.psum_scatter(partial_value.reshape(panels * tile_size, hidden), 'rep'...  25.9 us
    reduce_scatter x1, waiting for transfers between devices, on_device(): lax.psum_scatter(running.reshape(panels * tile_size, hidden), 'rep', scat...  24.9 us
    ppermute x6, starting transfers between devices, from_behind(): return lax.ppermute(value, axis, pairs)  18.5 us
    all_gather x1, blocking collectives, on_device(): lax.all_gather(agg_grad, 'rep', axis=0, tiled=True)  12.1 us
    unnamed x31, local copies, waits for them, and re-layouts  10.2 us
    convert_element_type x8, other arithmetic, source_parts(): active = (slot_ids < limit).astype(jnp.float32)[:, None, None]  6.74 us
  transfers between devices with their start and end apart: 9, of which 9 were waited for; matrix products, arithmetic and copies ran while one was open for 7% of the time, Pallas kernels for 0%

commit v1 on v0

v1 whole, which is shorter than its diff:
```python
import functools

import jax
import jax.numpy as jnp
from jax import lax
from jax.experimental import pallas as pl
from jax.experimental.pallas import tpu as pltpu
from jax.sharding import PartitionSpec as P

MESH = pl.DeviceIdType.MESH
HALVES = 2
F32 = jnp.float32
BF16 = jnp.bfloat16
GELU_SCALE = 0.7978845608028654
GELU_CUBIC = 0.044715


def dot(left, right, left_dim, right_dim):
    return lax.dot_general(
        left, right, (((left_dim,), (right_dim,)), ((), ())), preferred_element_type=F32
    )


def layer_kernel(
    n_blk, n_rep,
    feat, weight, cot, tiles, rows, cols, count, cols_vec,
    out, fgrad, wgrad,
    idx_vec, idx, fsend, frecv, acc, rsend, rrecv, agg, grad0, grad1,
    bsend, brecv, facc, qsend, qrecv, wlocal, wrecv, wrep,
    idx_send, idx_recv, idx_local, f_send, f_recv, r_send, r_recv, g_send, g_recv,
    b_send, b_recv, q_send, q_recv, w1_send, w1_recv, w2_send, w2_recv, w3_send, w3_recv,
):
    tile = tiles.shape[-1]
    slots = tiles.shape[1]
    panels = feat.shape[0]
    hidden = feat.shape[2]
    width = hidden // HALVES
    chunk = panels * tile // n_rep
    per_panel = tile // chunk
    wchunk = hidden // n_blk
    chips = n_blk // 2
    blk = lax.axis_index("blk")
    rep = lax.axis_index("rep")
    chip, core = blk // 2, blk % 2
    grads = (grad0, grad1)

    def blk_to(j):
        return ((chip + j // 2) % chips) * 2 + (core + j) % 2

    def blk_from(j):
        return ((chip + chips - j // 2) % chips) * 2 + (core + j) % 2

    def rep_to(k):
        return (rep + k) % n_rep

    def to_blk(j, src, dst, send_sem, recv_sem):
        return pltpu.make_async_remote_copy(
            src_ref=src, dst_ref=dst, send_sem=send_sem, recv_sem=recv_sem,
            device_id={"blk": blk_to(j)}, device_id_type=MESH,
        )

    def to_rep(k, src, dst, send_sem, recv_sem):
        return pltpu.make_async_remote_copy(
            src_ref=src, dst_ref=dst, send_sem=send_sem, recv_sem=recv_sem,
            device_id={"rep": rep_to(k)}, device_id_type=MESH,
        )

    def each(total, body):
        def step(at, carry):
            body(at)
            return carry
        if total <= 4:
            for at in range(1, total):
                body(at)
        else:
            lax.fori_loop(1, total, step, 0)

    def far_first(body):
        if n_blk <= 4:
            for j in list(range(2, n_blk)) + [1]:
                body(j)
        else:
            each(n_blk, body)

    my_part = pl.ds(pl.multiple_of((rep % per_panel) * chunk, chunk), chunk)

    def idx_copy(j):
        return to_blk(j, cols_vec, idx_vec.at[j], idx_send.at[j], idx_recv.at[j])

    def feat_copy(h, j):
        return to_blk(j, fsend.at[h, j], frecv.at[h, j], f_send.at[h, j], f_recv.at[h, j])

    def part_copy(h, k):
        rows_there = pl.ds(pl.multiple_of(rep_to(k) * chunk, chunk), chunk)
        return to_rep(k, rsend.at[h, rows_there], rrecv.at[h, k], r_send.at[h, k], r_recv.at[h, k])

    def grad_copy(h, k):
        here = grads[h].at[rep // per_panel, my_part]
        return to_rep(k, here, here, g_send.at[h, k], g_recv.at[h, k])

    def back_copy(h, j):
        return to_blk(j, bsend.at[h, j], brecv.at[h, j], b_send.at[h, j], b_recv.at[h, j])

    def fpart_copy(h, k):
        rows_there = pl.ds(pl.multiple_of(rep_to(k) * chunk, chunk), chunk)
        return to_rep(k, qsend.at[h, rows_there], qrecv.at[h, k], q_send.at[h, k], q_recv.at[h, k])

    def wpart_copy(j):
        there = pl.ds(pl.multiple_of(blk_to(j) * wchunk, wchunk), wchunk)
        return to_blk(j, wlocal.at[there], wrecv.at[j], w1_send.at[j], w1_recv.at[j])

    def wrep_copy(k):
        return to_rep(k, wrep.at[rep], wrep.at[rep], w2_send.at[k], w2_recv.at[k])

    wmine = pl.ds(pl.multiple_of(blk * wchunk, wchunk), wchunk)

    def wall_copy(j):
        return to_blk(j, wgrad.at[wmine], wgrad.at[wmine], w3_send.at[j], w3_recv.at[j])

    mine = pl.ds(pl.multiple_of(rep * chunk, chunk), chunk)

    barrier = pltpu.get_barrier_semaphore()

    def greet_blk(j):
        pl.semaphore_signal(barrier, inc=1, device_id={"blk": blk_to(j)}, device_id_type=MESH)

    def greet_rep(k):
        pl.semaphore_signal(barrier, inc=1, device_id={"rep": rep_to(k)}, device_id_type=MESH)

    each(n_blk, greet_blk)
    each(n_rep, greet_rep)
    pl.semaphore_wait(barrier, n_blk + n_rep - 2)

    far_first(lambda j: idx_copy(j).start())

    def in_use(owner, s):
        return s < count[0, 0, owner]

    def panel(p):
        return slice(p * tile, (p + 1) * tile)

    for s in range(slots):
        col = cols[blk, s]
        product = dot(tiles[blk, s], feat[col], 1, 0)
        for p in range(panels):
            keep = jnp.where((rows[blk, s] == p) & in_use(blk, s), 1.0, 0.0)
            for h in range(HALVES):
                piece = keep * product[:, h * width:(h + 1) * width]
                acc[h, panel(p), :] = piece if s == 0 else acc[h, panel(p), :] + piece

    def take_idx(j):
        idx_copy(j).wait_recv()
        local = pltpu.make_async_copy(idx_vec.at[j], idx.at[j], idx_local.at[j])
        local.start()
        local.wait()

    each(n_blk, take_idx)

    for h in range(HALVES):
        def serve(j, h=h):
            for s in range(slots):
                col = idx[j, blk, s]
                fsend[h, opposite(j), s] = feat[col][:, h * width:(h + 1) * width]
            feat_copy(h, opposite(j)).start()

        def opposite(j):
            return ((chips - j // 2) % chips) * 2 + j % 2

        far_first(serve)

    for h in range(HALVES):
        def absorb(j, h=h):
            feat_copy(h, j).wait_recv()
            owner = blk_from(j)
            products = [dot(tiles[owner, s], frecv[h, j, s], 1, 0) for s in range(slots)]
            for p in range(panels):
                total = acc[h, panel(p), :]
                for s in range(slots):
                    keep = jnp.where((rows[owner, s] == p) & in_use(owner, s), 1.0, 0.0)
                    total = total + keep * products[s]
                acc[h, panel(p), :] = total

        each(n_blk, absorb)
        rsend[h] = acc[h].astype(BF16)
        each(n_rep, lambda k, h=h: part_copy(h, k).start())

    for h in range(HALVES):
        each(n_rep, lambda k, h=h: part_copy(h, k).wait_recv())
        total = acc[h, mine, :]
        for k in range(1, n_rep):
            total = total + rrecv[h, k].astype(F32)
        agg[:, h * width:(h + 1) * width] = total.astype(BF16)

    pre_act = dot(agg[...], weight[...], 1, 0)
    bent = jnp.tanh(GELU_SCALE * (pre_act + GELU_CUBIC * pre_act * pre_act * pre_act))
    out[...] = (0.5 * pre_act * (1.0 + bent)).astype(BF16)
    slope = 0.5 * (1.0 + bent) + 0.5 * pre_act * (1.0 - bent * bent) * GELU_SCALE * (
        1.0 + 3.0 * GELU_CUBIC * pre_act * pre_act
    )
    pre_grad = (cot[...].astype(F32) * slope).astype(BF16)
    agg_grad = dot(pre_grad, weight[...], 1, 1).astype(BF16)
    for h in range(HALVES):
        grads[h][rep // per_panel, my_part, :] = agg_grad[:, h * width:(h + 1) * width]
        each(n_rep, lambda k, h=h: grad_copy(h, k).start())

    wlocal[...] = dot(agg[...], pre_grad, 0, 0)
    far_first(lambda j: wpart_copy(j).start())

    def back_product(h, owner, s):
        return dot(tiles[owner, s], grads[h][rows[owner, s]], 0, 0)

    for h in range(HALVES):
        each(n_rep, lambda k, h=h: grad_copy(h, k).wait_recv())

        def give(j, h=h):
            owner = blk_to(j)
            for s in range(slots):
                keep = jnp.where(in_use(owner, s), 1.0, 0.0)
                bsend[h, j, s] = (keep * back_product(h, owner, s)).astype(BF16)
            back_copy(h, j).start()

        far_first(give)

    wtotal = wlocal[wmine, :]
    each(n_blk, lambda j: wpart_copy(j).wait_recv())
    for j in range(1, n_blk):
        wtotal = wtotal + wrecv[j]
    wrep[rep] = wtotal
    each(n_rep, lambda k: wrep_copy(k).start())

    for h in range(HALVES):
        for s in range(slots):
            product = back_product(h, blk, s)
            for p in range(panels):
                keep = jnp.where((cols[blk, s] == p) & in_use(blk, s), 1.0, 0.0)
                piece = keep * product
                facc[h, panel(p), :] = piece if s == 0 else facc[h, panel(p), :] + piece

    for h in range(HALVES):
        def collect(j, h=h):
            back_copy(h, j).wait_recv()
            for p in range(panels):
                total = facc[h, panel(p), :]
                for s in range(slots):
                    keep = jnp.where(idx[j, blk, s] == p, 1.0, 0.0)
                    total = total + keep * brecv[h, j, s].astype(F32)
                facc[h, panel(p), :] = total

        each(n_blk, collect)
        qsend[h] = facc[h].astype(BF16)
        each(n_rep, lambda k, h=h: fpart_copy(h, k).start())
        if h == 0:
            each(n_rep, lambda k: wrep_copy(k).wait_recv())
            wtotal = wrep[0]
            for k in range(1, n_rep):
                wtotal = wtotal + wrep[k]
            wgrad[wmine, :] = wtotal
            far_first(lambda j: wall_copy(j).start())

    for h in range(HALVES):
        each(n_rep, lambda k, h=h: fpart_copy(h, k).wait_recv())
        total = facc[h, mine, :]
        for k in range(1, n_rep):
            total = total + qrecv[h, k].astype(F32)
        fgrad[:, h * width:(h + 1) * width] = total.astype(BF16)

    def finish_blk(j):
        wall_copy(j).wait_recv()
        idx_copy(j).wait_send()
        wpart_copy(j).wait_send()
        wall_copy(j).wait_send()
        for h in range(HALVES):
            feat_copy(h, j).wait_send()
            back_copy(h, j).wait_send()

    def finish_rep(k):
        wrep_copy(k).wait_send()
        for h in range(HALVES):
            part_copy(h, k).wait_send()
            grad_copy(h, k).wait_send()
            fpart_copy(h, k).wait_send()

    each(n_blk, finish_blk)
    each(n_rep, finish_rep)


def on_device(features, weight, cotangent, tiles, tile_rows, tile_cols, tile_count):
    n_blk, n_rep = lax.axis_size("blk"), lax.axis_size("rep")
    nodes, hidden = features.shape
    slots, tile = tiles.shape[3], tiles.shape[-1]
    width, chunk, wchunk = hidden // HALVES, nodes // n_rep, hidden // n_blk
    cols = tile_cols.reshape(n_blk, slots)
    vmem = pl.BlockSpec(memory_space=pltpu.VMEM)
    smem = pl.BlockSpec(memory_space=pltpu.SMEM)
    dma = pltpu.SemaphoreType.DMA
    by_blk, by_rep = dma((HALVES, n_blk)), dma((HALVES, n_rep))
    return pl.pallas_call(
        functools.partial(layer_kernel, n_blk, n_rep),
        out_shape=(
            jax.ShapeDtypeStruct((chunk, hidden), BF16),
            jax.ShapeDtypeStruct((chunk, hidden), BF16),
            jax.ShapeDtypeStruct((hidden, hidden), F32),
        ),
        in_specs=[vmem, vmem, vmem, vmem, smem, smem, smem, vmem],
        out_specs=(vmem, vmem, vmem),
        scratch_shapes=[
            pltpu.VMEM((n_blk, n_blk, slots), jnp.int32),
            pltpu.SMEM((n_blk, n_blk, slots), jnp.int32),
            pltpu.VMEM((HALVES, n_blk, slots, tile, width), BF16),
            pltpu.VMEM((HALVES, n_blk, slots, tile, width), BF16),
            pltpu.VMEM((HALVES, nodes, width), F32),
            pltpu.VMEM((HALVES, nodes, width), BF16),
            pltpu.VMEM((HALVES, n_rep, chunk, width), BF16),
            pltpu.VMEM((chunk, hidden), BF16),
            pltpu.VMEM((nodes // tile, tile, width), BF16),
            pltpu.VMEM((nodes // tile, tile, width), BF16),
            pltpu.VMEM((HALVES, n_blk, slots, tile, width), BF16),
            pltpu.VMEM((HALVES, n_blk, slots, tile, width), BF16),
            pltpu.VMEM((HALVES, nodes, width), F32),
            pltpu.VMEM((HALVES, nodes, width), BF16),
            pltpu.VMEM((HALVES, n_rep, chunk, width), BF16),
            pltpu.VMEM((hidden, hidden), F32),
            pltpu.VMEM((n_blk, wchunk, hidden), F32),
            pltpu.VMEM((n_rep, wchunk, hidden), F32),
            dma((n_blk,)), dma((n_blk,)), dma((n_blk,)),
            by_blk, by_blk, by_rep, by_rep, by_rep, by_rep,
            by_blk, by_blk, by_rep, by_rep,
            dma((n_blk,)), dma((n_blk,)), dma((n_rep,)), dma((n_rep,)), dma((n_blk,)), dma((n_blk,)),
        ],
        compiler_params=pltpu.CompilerParams(
            collective_id=0, has_side_effects=True, vmem_limit_bytes=56 * 1024 * 1024
        ),
    )(
        features.reshape(nodes // tile, tile, hidden), weight, cotangent, tiles.reshape(n_blk, slots, tile, tile),
        tile_rows.reshape(n_blk, slots), cols, tile_count, cols,
    )


def solution(mesh):
    in_specs = (
        P(("groups", "blk"), None),
        P(),
        P(("groups", "blk", "rep"), None),
        P(("groups", "blk"), "rep", None, None, None, None),
        P(("groups", "blk"), "rep", None, None),
        P(("groups", "blk"), "rep", None, None),
        P(("groups", "blk"), "rep", None),
    )
    out_specs = (
        P(("groups", "blk", "rep"), None),
        P(("groups", "blk", "rep"), None),
        P("groups", None),
    )
    return jax.shard_map(
        on_device, mesh=mesh, in_specs=in_specs, out_specs=out_specs, check_vma=False
    )
```

time: 275 us -> 68.3 us (0.25)
  the two profiles are of different devices: /device:TPU:1 before, /device:TPU:0 now
where the time goes in v1:
time: 68.3 us; the launch traced here: 68.1 us
  Pallas kernels  62.5 us (92%)
  local copies, waits for them, and re-layouts  5 us (7%)
    pallas_call x1, Pallas kernels, on_device(): pl.pallas_call(functools.partial(layer_kernel, n_blk, n_rep), out_shape=(...  62.5 us
    unnamed x11, local copies, waits for them, and re-layouts  3.67 us

profile of v1, /device:TPU:0, one launch (start us, length us, event | category | flops | bytes accessed | tf_op | source)
XLA Modules:
  0.0 68.1 jit_solution(17882941648204219134)
XLA Ops:
  0.6 0.0 copy-start.2
  0.6 0.7 copy-done.2
  1.3 0.0 copy-start.3
  1.3 0.7 copy.10.rows
  2.0 0.0 copy-done.3
  2.0 0.7 copy.11.cols.cols_vec
  2.7 62.5 %shard_map.94 = (bf16[256,256]{1,0:T(8,128)(2,1)}, bf16[256,256]{1,0:T(8,128)(2,1)}, f32[256,256]{1,0:T(8,128)}) custom-call(bf16[4,256,256]{2,1,0:T(8,128)(2,1)} %bitcast.5, bf16[256,256]{1,0:T(8,128)(2,1)} %weight.1, bf16[256,256]{1,0:T(8,128)(2,1)} %cot.1, bf16[4,2,256,256]{3,2,1,0:T(8,128)(2,1)} %bitcast.4, s32[4,2]{1,0:T(4,128)} %copy.10.rows, ...), custom_call_target="tpu_custom_call" | custom-call | tf_op jit(solution)/shard_map/pallas_call | solution.py:297
  65.1 0.0 copy-start.1
  65.2 0.0 copy-start
  65.2 1.6 %copy.16 = bf16[256,256]{1,0:T(8,128)(2,1)} copy(bf16[256,256]{1,0:T(8,128)(2,1)} %get-tuple-element.6) | data formatting | bytes 262144
  66.8 0.0 copy-done.1
  66.8 0.7 copy.17
  67.4 0.0 copy-done
  67.4 0.7 %copy.18 = f32[256,256]{1,0:T(8,128)} copy(f32[256,256]{1,0:T(8,128)S(1)} %copy-done) | data formatting | bytes 524288
Async XLA Ops:
  0.6 0.7 copy-start.2
  1.3 0.7 copy-start.3
  65.1 1.6 %copy-start.1 = (bf16[256,256]{1,0:T(8,128)(2,1)S(1)}, bf16[256,256]{1,0:T(8,128)(2,1)}, u32[]{:S(2)}) copy-start(bf16[256,256]{1,0:T(8,128)(2,1)} %get-tuple-element.7) | copy-start | bytes 393220
  65.2 2.3 %copy-start = (f32[256,256]{1,0:T(8,128)S(1)}, f32[256,256]{1,0:T(8,128)}, u32[]{:S(2)}) copy-start(f32[256,256]{1,0:T(8,128)} %get-tuple-element.8) | copy-start | bytes 786436

commit v2 on v1

--- a/solution.py
+++ b/solution.py
@@ -140,10 +140,10 @@
         return slice(p * tile, (p + 1) * tile)
 
     for s in range(slots):
-        col = cols[blk, s]
+        col = cols[s, blk]
         product = dot(tiles[blk, s], feat[col], 1, 0)
         for p in range(panels):
-            keep = jnp.where((rows[blk, s] == p) & in_use(blk, s), 1.0, 0.0)
+            keep = jnp.where((rows[s, blk] == p) & in_use(blk, s), 1.0, 0.0)
             for h in range(HALVES):
                 piece = keep * product[:, h * width:(h + 1) * width]
                 acc[h, panel(p), :] = piece if s == 0 else acc[h, panel(p), :] + piece
@@ -156,10 +156,11 @@
 
     each(n_blk, take_idx)
 
+
     for h in range(HALVES):
         def serve(j, h=h):
             for s in range(slots):
-                col = idx[j, blk, s]
+                col = idx[j, s, blk]
                 fsend[h, opposite(j), s] = feat[col][:, h * width:(h + 1) * width]
             feat_copy(h, opposite(j)).start()
 
@@ -176,7 +177,7 @@
             for p in range(panels):
                 total = acc[h, panel(p), :]
                 for s in range(slots):
-                    keep = jnp.where((rows[owner, s] == p) & in_use(owner, s), 1.0, 0.0)
+                    keep = jnp.where((rows[s, owner] == p) & in_use(owner, s), 1.0, 0.0)
                     total = total + keep * products[s]
                 acc[h, panel(p), :] = total
 
@@ -207,7 +208,7 @@
     far_first(lambda j: wpart_copy(j).start())
 
     def back_product(h, owner, s):
-        return dot(tiles[owner, s], grads[h][rows[owner, s]], 0, 0)
+        return dot(tiles[owner, s], grads[h][rows[s, owner]], 0, 0)
 
     for h in range(HALVES):
         each(n_rep, lambda k, h=h: grad_copy(h, k).wait_recv())
@@ -232,7 +233,7 @@
         for s in range(slots):
             product = back_product(h, blk, s)
             for p in range(panels):
-                keep = jnp.where((cols[blk, s] == p) & in_use(blk, s), 1.0, 0.0)
+                keep = jnp.where((cols[s, blk] == p) & in_use(blk, s), 1.0, 0.0)
                 piece = keep * product
                 facc[h, panel(p), :] = piece if s == 0 else facc[h, panel(p), :] + piece
 
@@ -242,7 +243,7 @@
             for p in range(panels):
                 total = facc[h, panel(p), :]
                 for s in range(slots):
-                    keep = jnp.where(idx[j, blk, s] == p, 1.0, 0.0)
+                    keep = jnp.where(idx[j, s, blk] == p, 1.0, 0.0)
                     total = total + keep * brecv[h, j, s].astype(F32)
                 facc[h, panel(p), :] = total
 
@@ -284,17 +285,23 @@
     each(n_rep, finish_rep)
 
 
+def hand_over(out_in, fgrad_in, wgrad_in, out, fgrad, wgrad):
+    out[...] = out_in[...]
+    fgrad[...] = fgrad_in[...]
+    wgrad[...] = wgrad_in[...]
+
+
 def on_device(features, weight, cotangent, tiles, tile_rows, tile_cols, tile_count):
     n_blk, n_rep = lax.axis_size("blk"), lax.axis_size("rep")
     nodes, hidden = features.shape
     slots, tile = tiles.shape[3], tiles.shape[-1]
     width, chunk, wchunk = hidden // HALVES, nodes // n_rep, hidden // n_blk
-    cols = tile_cols.reshape(n_blk, slots)
+    cols = tile_cols[0, 0].T
     vmem = pl.BlockSpec(memory_space=pltpu.VMEM)
     smem = pl.BlockSpec(memory_space=pltpu.SMEM)
     dma = pltpu.SemaphoreType.DMA
     by_blk, by_rep = dma((HALVES, n_blk)), dma((HALVES, n_rep))
-    return pl.pallas_call(
+    results = pl.pallas_call(
         functools.partial(layer_kernel, n_blk, n_rep),
         out_shape=(
             jax.ShapeDtypeStruct((chunk, hidden), BF16),
@@ -304,8 +311,8 @@
         in_specs=[vmem, vmem, vmem, vmem, smem, smem, smem, vmem],
         out_specs=(vmem, vmem, vmem),
         scratch_shapes=[
-            pltpu.VMEM((n_blk, n_blk, slots), jnp.int32),
-            pltpu.SMEM((n_blk, n_blk, slots), jnp.int32),
+            pltpu.VMEM((n_blk, slots, n_blk), jnp.int32),
+            pltpu.SMEM((n_blk, slots, n_blk), jnp.int32),
             pltpu.VMEM((HALVES, n_blk, slots, tile, width), BF16),
             pltpu.VMEM((HALVES, n_blk, slots, tile, width), BF16),
             pltpu.VMEM((HALVES, nodes, width), F32),
@@ -332,8 +339,14 @@
         ),
     )(
         features.reshape(nodes // tile, tile, hidden), weight, cotangent, tiles.reshape(n_blk, slots, tile, tile),
-        tile_rows.reshape(n_blk, slots), cols, tile_count, cols,
-    )
+        tile_rows[0, 0].T, cols, tile_count, cols,
+    )
+    return pl.pallas_call(
+        hand_over,
+        out_shape=tuple(jax.ShapeDtypeStruct(r.shape, r.dtype) for r in results),
+        in_specs=[vmem] * 3,
+        out_specs=(vmem, vmem, vmem),
+    )(*results)
 
 
 def solution(mesh):

time: 68.3 us -> 64.2 us (0.940)
  the two profiles are of different devices: /device:TPU:0 before, /device:TPU:1 now
where the time goes in v2:
time: 64.2 us; the launch traced here: 63.8 us
  Pallas kernels  63.2 us (98%)
    pallas_call x1, Pallas kernels, on_device(): pl.pallas_call(functools.partial(layer_kernel, n_blk, n_rep), out_shape=(...  61.3 us
    pallas_call x1, Pallas kernels, on_device(): pl.pallas_call(hand_over, out_shape=tuple((jax.ShapeDtypeStruct(r.shape,...  1.88 us

profile of v2, /device:TPU:1, one launch (start us, length us, event | category | flops | bytes accessed | tf_op | source)
XLA Modules:
  0.0 63.8 jit_solution(4457855385940057200)
XLA Ops:
  0.6 61.3 %shard_map.94 = (bf16[256,256]{1,0:T(8,128)(2,1)}, bf16[256,256]{1,0:T(8,128)(2,1)}, f32[256,256]{1,0:T(8,128)}) custom-call(bf16[4,256,256]{2,1,0:T(8,128)(2,1)} %bitcast.9, bf16[256,256]{1,0:T(8,128)(2,1)} %weight.1, bf16[256,256]{1,0:T(8,128)(2,1)} %cot.1, bf16[4,2,256,256]{3,2,1,0:T(8,128)(2,1)} %bitcast.8, s32[2,4]{1,0:T(2,128)} %bitcast.12, ...), custom_call_target="tpu_custom_call" | custom-call | tf_op jit(solution)/shard_map/pallas_call | solution.py:304
  61.9 1.9 %shard_map.95 = (bf16[256,256]{1,0:T(8,128)(2,1)}, bf16[256,256]{1,0:T(8,128)(2,1)}, f32[256,256]{1,0:T(8,128)}) custom-call(bf16[256,256]{1,0:T(8,128)(2,1)} %get-tuple-element.6.out_in, bf16[256,256]{1,0:T(8,128)(2,1)} %get-tuple-element.7.fgrad_in, f32[256,256]{1,0:T(8,128)} %get-tuple-element.8.wgrad_in), custom_call_target="tpu_custom_call" | custom-call | tf_op jit(solution)/shard_map/pallas_call | solution.py:344

commit v3 on v2

--- a/solution.py
+++ b/solution.py
@@ -23,9 +23,9 @@
 
 def layer_kernel(
     n_blk, n_rep,
-    feat, weight, cot, tiles, rows, cols, count, cols_vec,
+    feat_in, weight_in, cot_in, tiles_in, rows, cols, count, cols_vec,
     out, fgrad, wgrad,
-    idx_vec, idx, fsend, frecv, acc, rsend, rrecv, agg, grad0, grad1,
+    feat, weight, cot, tiles, load, far, idx_vec, idx, acc, rsend, rrecv, agg, grad0, grad1,
     bsend, brecv, facc, qsend, qrecv, wlocal, wrecv, wrep,
     idx_send, idx_recv, idx_local, f_send, f_recv, r_send, r_recv, g_send, g_recv,
     b_send, b_recv, q_send, q_recv, w1_send, w1_recv, w2_send, w2_recv, w3_send, w3_recv,
@@ -88,7 +88,11 @@
         return to_blk(j, cols_vec, idx_vec.at[j], idx_send.at[j], idx_recv.at[j])
 
     def feat_copy(h, j):
-        return to_blk(j, fsend.at[h, j], frecv.at[h, j], f_send.at[h, j], f_recv.at[h, j])
+        half = feat.at[:, :, h * width:(h + 1) * width]
+        return to_blk(j, half, far[h][j - 1], f_send.at[h, j], f_recv.at[h, j])
+
+    def pass_on(h, j):
+        return to_blk(1, far[h][j - 1], far[h][j], f_send.at[h, j + 1], f_recv.at[h, j + 1])
 
     def part_copy(h, k):
         rows_there = pl.ds(pl.multiple_of(rep_to(k) * chunk, chunk), chunk)
@@ -119,6 +123,15 @@
 
     mine = pl.ds(pl.multiple_of(rep * chunk, chunk), chunk)
 
+    loads = [
+        pltpu.make_async_copy(src, dst, load.at[at])
+        for at, (src, dst) in enumerate(
+            ((feat_in, feat), (tiles_in, tiles), (weight_in, weight), (cot_in, cot))
+        )
+    ]
+    for copy in loads:
+        copy.start()
+
     barrier = pltpu.get_barrier_semaphore()
 
     def greet_blk(j):
@@ -131,7 +144,13 @@
     each(n_rep, greet_rep)
     pl.semaphore_wait(barrier, n_blk + n_rep - 2)
 
+    loads[0].wait()
+    for h in range(HALVES):
+        for j in list(range(2, n_blk, 2)) + [1]:
+            feat_copy(h, j).start()
     far_first(lambda j: idx_copy(j).start())
+    for copy in loads[1:]:
+        copy.wait()
 
     def in_use(owner, s):
         return s < count[0, 0, owner]
@@ -148,32 +167,10 @@
                 piece = keep * product[:, h * width:(h + 1) * width]
                 acc[h, panel(p), :] = piece if s == 0 else acc[h, panel(p), :] + piece
 
-    def take_idx(j):
-        idx_copy(j).wait_recv()
-        local = pltpu.make_async_copy(idx_vec.at[j], idx.at[j], idx_local.at[j])
-        local.start()
-        local.wait()
-
-    each(n_blk, take_idx)
-
-
-    for h in range(HALVES):
-        def serve(j, h=h):
-            for s in range(slots):
-                col = idx[j, s, blk]
-                fsend[h, opposite(j), s] = feat[col][:, h * width:(h + 1) * width]
-            feat_copy(h, opposite(j)).start()
-
-        def opposite(j):
-            return ((chips - j // 2) % chips) * 2 + j % 2
-
-        far_first(serve)
-
     for h in range(HALVES):
         def absorb(j, h=h):
-            feat_copy(h, j).wait_recv()
             owner = blk_from(j)
-            products = [dot(tiles[owner, s], frecv[h, j, s], 1, 0) for s in range(slots)]
+            products = [dot(tiles[owner, s], far[h][j - 1][cols[s, owner]], 1, 0) for s in range(slots)]
             for p in range(panels):
                 total = acc[h, panel(p), :]
                 for s in range(slots):
@@ -181,7 +178,15 @@
                     total = total + keep * products[s]
                 acc[h, panel(p), :] = total
 
-        each(n_blk, absorb)
+        feat_copy(h, 1).wait_recv()
+        absorb(1)
+        for j in range(2, n_blk, 2):
+            feat_copy(h, j).wait_recv()
+            pass_on(h, j).start()
+            absorb(j)
+        for j in range(2, n_blk, 2):
+            pass_on(h, j).wait_recv()
+            absorb(j + 1)
         rsend[h] = acc[h].astype(BF16)
         each(n_rep, lambda k, h=h: part_copy(h, k).start())
 
@@ -206,6 +211,14 @@
 
     wlocal[...] = dot(agg[...], pre_grad, 0, 0)
     far_first(lambda j: wpart_copy(j).start())
+
+    def take_idx(j):
+        idx_copy(j).wait_recv()
+        local = pltpu.make_async_copy(idx_vec.at[j], idx.at[j], idx_local.at[j])
+        local.start()
+        local.wait()
+
+    each(n_blk, take_idx)
 
     def back_product(h, owner, s):
         return dot(tiles[owner, s], grads[h][rows[s, owner]], 0, 0)
@@ -221,13 +234,13 @@
             back_copy(h, j).start()
 
         far_first(give)
-
-    wtotal = wlocal[wmine, :]
-    each(n_blk, lambda j: wpart_copy(j).wait_recv())
-    for j in range(1, n_blk):
-        wtotal = wtotal + wrecv[j]
-    wrep[rep] = wtotal
-    each(n_rep, lambda k: wrep_copy(k).start())
+        if h == 0:
+            wtotal = wlocal[wmine, :]
+            each(n_blk, lambda j: wpart_copy(j).wait_recv())
+            for j in range(1, n_blk):
+                wtotal = wtotal + wrecv[j]
+            wrep[rep] = wtotal.astype(BF16)
+            each(n_rep, lambda k: wrep_copy(k).start())
 
     for h in range(HALVES):
         for s in range(slots):
@@ -252,9 +265,9 @@
         each(n_rep, lambda k, h=h: fpart_copy(h, k).start())
         if h == 0:
             each(n_rep, lambda k: wrep_copy(k).wait_recv())
-            wtotal = wrep[0]
+            wtotal = wrep[0].astype(F32)
             for k in range(1, n_rep):
-                wtotal = wtotal + wrep[k]
+                wtotal = wtotal + wrep[k].astype(F32)
             wgrad[wmine, :] = wtotal
             far_first(lambda j: wall_copy(j).start())
 
@@ -271,7 +284,6 @@
         wpart_copy(j).wait_send()
         wall_copy(j).wait_send()
         for h in range(HALVES):
-            feat_copy(h, j).wait_send()
             back_copy(h, j).wait_send()
 
     def finish_rep(k):
@@ -281,6 +293,11 @@
             grad_copy(h, k).wait_send()
             fpart_copy(h, k).wait_send()
 
+    for h in range(HALVES):
+        for j in list(range(2, n_blk, 2)) + [1]:
+            feat_copy(h, j).wait_send()
+        for j in range(2, n_blk, 2):
+            pass_on(h, j).wait_send()
     each(n_blk, finish_blk)
     each(n_rep, finish_rep)
 
@@ -295,10 +312,12 @@
     n_blk, n_rep = lax.axis_size("blk"), lax.axis_size("rep")
     nodes, hidden = features.shape
     slots, tile = tiles.shape[3], tiles.shape[-1]
+    panels = nodes // tile
     width, chunk, wchunk = hidden // HALVES, nodes // n_rep, hidden // n_blk
     cols = tile_cols[0, 0].T
     vmem = pl.BlockSpec(memory_space=pltpu.VMEM)
     smem = pl.BlockSpec(memory_space=pltpu.SMEM)
+    whole = pl.BlockSpec(memory_space=pl.ANY)
     dma = pltpu.SemaphoreType.DMA
     by_blk, by_rep = dma((HALVES, n_blk)), dma((HALVES, n_rep))
     results = pl.pallas_call(
@@ -308,13 +327,17 @@
             jax.ShapeDtypeStruct((chunk, hidden), BF16),
             jax.ShapeDtypeStruct((hidden, hidden), F32),
         ),
-        in_specs=[vmem, vmem, vmem, vmem, smem, smem, smem, vmem],
+        in_specs=[whole, whole, whole, whole, smem, smem, smem, vmem],
         out_specs=(vmem, vmem, vmem),
         scratch_shapes=[
+            pltpu.VMEM((panels, tile, hidden), BF16),
+            pltpu.VMEM((hidden, hidden), BF16),
+            pltpu.VMEM((chunk, hidden), BF16),
+            pltpu.VMEM((n_blk, slots, tile, tile), BF16),
+            dma((4,)),
+            [[pltpu.VMEM((panels, tile, width), BF16)] * (n_blk - 1)] * HALVES,
             pltpu.VMEM((n_blk, slots, n_blk), jnp.int32),
             pltpu.SMEM((n_blk, slots, n_blk), jnp.int32),
-            pltpu.VMEM((HALVES, n_blk, slots, tile, width), BF16),
-            pltpu.VMEM((HALVES, n_blk, slots, tile, width), BF16),
             pltpu.VMEM((HALVES, nodes, width), F32),
             pltpu.VMEM((HALVES, nodes, width), BF16),
             pltpu.VMEM((HALVES, n_rep, chunk, width), BF16),
@@ -328,7 +351,7 @@
             pltpu.VMEM((HALVES, n_rep, chunk, width), BF16),
             pltpu.VMEM((hidden, hidden), F32),
             pltpu.VMEM((n_blk, wchunk, hidden), F32),
-            pltpu.VMEM((n_rep, wchunk, hidden), F32),
+            pltpu.VMEM((n_rep, wchunk, hidden), BF16),
             dma((n_blk,)), dma((n_blk,)), dma((n_blk,)),
             by_blk, by_blk, by_rep, by_rep, by_rep, by_rep,
             by_blk, by_blk, by_rep, by_rep,

time: 64.2 us -> 59.8 us (0.931)
  Pallas kernels: 63.2 us -> 58.9 us
    pallas_call x1, Pallas kernels: 61.3 us -> 57 us  [on_device(): pl.pallas_call(functools.partial(layer_kernel, n_blk, n_rep), out_shape=(...]
where the time goes in v3:
time: 59.8 us; the launch traced here: 59.6 us
  Pallas kernels  58.9 us (98%)
  between operations  0.64 us (1%)
    pallas_call x1, Pallas kernels, on_device(): pl.pallas_call(functools.partial(layer_kernel, n_blk, n_rep), out_shape=(...  57 us
    pallas_call x1, Pallas kernels, on_device(): pl.pallas_call(hand_over, out_shape=tuple((jax.ShapeDtypeStruct(r.shape,...  1.88 us

profile of v3, /device:TPU:1, one launch (start us, length us, event | category | flops | bytes accessed | tf_op | source)
XLA Modules:
  0.0 59.6 jit_solution(2056629075097377162)
XLA Ops:
  0.6 57.0 %shard_map.94 = (bf16[256,256]{1,0:T(8,128)(2,1)}, bf16[256,256]{1,0:T(8,128)(2,1)}, f32[256,256]{1,0:T(8,128)}) custom-call(bf16[4,256,256]{2,1,0:T(8,128)(2,1)} %bitcast.9, bf16[256,256]{1,0:T(8,128)(2,1)} %weight_in.1, bf16[256,256]{1,0:T(8,128)(2,1)} %cot_in.1, bf16[4,2,256,256]{3,2,1,0:T(8,128)(2,1)} %bitcast.8, s32[2,4]{1,0:T(2,128)} %bitcast.12, ...), custom_call_target="tpu_custom_call" | custom-call | tf_op jit(solution)/shard_map/pallas_call | solution.py:323
  57.7 1.9 %shard_map.95 = (bf16[256,256]{1,0:T(8,128)(2,1)}, bf16[256,256]{1,0:T(8,128)(2,1)}, f32[256,256]{1,0:T(8,128)}) custom-call(bf16[256,256]{1,0:T(8,128)(2,1)} %get-tuple-element.6.out_in, bf16[256,256]{1,0:T(8,128)(2,1)} %get-tuple-element.7.fgrad_in, f32[256,256]{1,0:T(8,128)} %get-tuple-element.8.wgrad_in), custom_call_target="tpu_custom_call" | custom-call | tf_op jit(solution)/shard_map/pallas_call | solution.py:367

commit v4 on v3

--- a/solution.py
+++ b/solution.py
@@ -9,6 +9,7 @@
 
 MESH = pl.DeviceIdType.MESH
 HALVES = 2
+STRIPS = 1
 F32 = jnp.float32
 BF16 = jnp.bfloat16
 GELU_SCALE = 0.7978845608028654
@@ -25,7 +26,7 @@
     n_blk, n_rep,
     feat_in, weight_in, cot_in, tiles_in, rows, cols, count, cols_vec,
     out, fgrad, wgrad,
-    feat, weight, cot, tiles, load, far, idx_vec, idx, acc, rsend, rrecv, agg, grad0, grad1,
+    feat, weight, cot, tiles, load, far, idx_vec, idx, acc, rsend, rrecv, agg, pre_grad, grad0, grad1,
     bsend, brecv, facc, qsend, qrecv, wlocal, wrecv, wrep,
     idx_send, idx_recv, idx_local, f_send, f_recv, r_send, r_recv, g_send, g_recv,
     b_send, b_recv, q_send, q_recv, w1_send, w1_recv, w2_send, w2_recv, w3_send, w3_recv,
@@ -37,6 +38,7 @@
     width = hidden // HALVES
     chunk = panels * tile // n_rep
     per_panel = tile // chunk
+    strip = chunk // STRIPS
     wchunk = hidden // n_blk
     chips = n_blk // 2
     blk = lax.axis_index("blk")
@@ -82,8 +84,6 @@
         else:
             each(n_blk, body)
 
-    my_part = pl.ds(pl.multiple_of((rep % per_panel) * chunk, chunk), chunk)
-
     def idx_copy(j):
         return to_blk(j, cols_vec, idx_vec.at[j], idx_send.at[j], idx_recv.at[j])
 
@@ -94,13 +94,17 @@
     def pass_on(h, j):
         return to_blk(1, far[h][j - 1], far[h][j], f_send.at[h, j + 1], f_recv.at[h, j + 1])
 
-    def part_copy(h, k):
-        rows_there = pl.ds(pl.multiple_of(rep_to(k) * chunk, chunk), chunk)
-        return to_rep(k, rsend.at[h, rows_there], rrecv.at[h, k], r_send.at[h, k], r_recv.at[h, k])
-
-    def grad_copy(h, k):
-        here = grads[h].at[rep // per_panel, my_part]
-        return to_rep(k, here, here, g_send.at[h, k], g_recv.at[h, k])
+    def part_copy(h, k, t):
+        rows_there = pl.ds(pl.multiple_of(rep_to(k) * chunk + t * strip, strip), strip)
+        lands = rrecv.at[h, k, pl.ds(t * strip, strip)]
+        return to_rep(k, rsend.at[h, rows_there], lands, r_send.at[h, k, t], r_recv.at[h, k, t])
+
+    def my_strip(t):
+        return pl.ds(pl.multiple_of((rep % per_panel) * chunk + t * strip, strip), strip)
+
+    def grad_copy(h, k, t):
+        here = grads[h].at[rep // per_panel, my_strip(t)]
+        return to_rep(k, here, here, g_send.at[h, k, t], g_recv.at[h, k, t])
 
     def back_copy(h, j):
         return to_blk(j, bsend.at[h, j], brecv.at[h, j], b_send.at[h, j], b_recv.at[h, j])
@@ -188,28 +192,41 @@
             pass_on(h, j).wait_recv()
             absorb(j + 1)
         rsend[h] = acc[h].astype(BF16)
-        each(n_rep, lambda k, h=h: part_copy(h, k).start())
-
-    for h in range(HALVES):
-        each(n_rep, lambda k, h=h: part_copy(h, k).wait_recv())
-        total = acc[h, mine, :]
+        for t in range(STRIPS):
+            each(n_rep, lambda k, h=h, t=t: part_copy(h, k, t).start())
+
+    def gather_part(h, t):
+        each(n_rep, lambda k: part_copy(h, k, t).wait_recv())
+        here = slice(t * strip, (t + 1) * strip)
+        total = acc[h, pl.ds(pl.multiple_of(rep * chunk + t * strip, strip), strip), :]
         for k in range(1, n_rep):
-            total = total + rrecv[h, k].astype(F32)
-        agg[:, h * width:(h + 1) * width] = total.astype(BF16)
-
-    pre_act = dot(agg[...], weight[...], 1, 0)
-    bent = jnp.tanh(GELU_SCALE * (pre_act + GELU_CUBIC * pre_act * pre_act * pre_act))
-    out[...] = (0.5 * pre_act * (1.0 + bent)).astype(BF16)
-    slope = 0.5 * (1.0 + bent) + 0.5 * pre_act * (1.0 - bent * bent) * GELU_SCALE * (
-        1.0 + 3.0 * GELU_CUBIC * pre_act * pre_act
-    )
-    pre_grad = (cot[...].astype(F32) * slope).astype(BF16)
-    agg_grad = dot(pre_grad, weight[...], 1, 1).astype(BF16)
-    for h in range(HALVES):
-        grads[h][rep // per_panel, my_part, :] = agg_grad[:, h * width:(h + 1) * width]
-        each(n_rep, lambda k, h=h: grad_copy(h, k).start())
-
-    wlocal[...] = dot(agg[...], pre_grad, 0, 0)
+            total = total + rrecv[h, k, here].astype(F32)
+        agg[here, h * width:(h + 1) * width] = total.astype(BF16)
+
+    for h in range(HALVES - 1):
+        for t in range(STRIPS):
+            gather_part(h, t)
+
+    for t in range(STRIPS):
+        gather_part(HALVES - 1, t)
+        here = slice(t * strip, (t + 1) * strip)
+        pre_act = dot(agg[here, :], weight[...], 1, 0)
+        bent = jnp.tanh(GELU_SCALE * (pre_act + GELU_CUBIC * pre_act * pre_act * pre_act))
+        slope = 0.5 * (1.0 + bent) + 0.5 * pre_act * (1.0 - bent * bent) * GELU_SCALE * (
+            1.0 + 3.0 * GELU_CUBIC * pre_act * pre_act
+        )
+        strip_grad = (cot[here, :].astype(F32) * slope).astype(BF16)
+        agg_grad = dot(strip_grad, weight[...], 1, 1).astype(BF16)
+        for h in range(HALVES):
+            grads[h][rep // per_panel, my_strip(t), :] = agg_grad[:, h * width:(h + 1) * width]
+        each(n_rep, lambda k, t=t: grad_copy(0, k, t).start())
+        pre_grad[here, :] = strip_grad
+        out[here, :] = (0.5 * pre_act * (1.0 + bent)).astype(BF16)
+    for h in range(1, HALVES):
+        for t in range(STRIPS):
+            each(n_rep, lambda k, h=h, t=t: grad_copy(h, k, t).start())
+
+    wlocal[...] = dot(agg[...], pre_grad[...], 0, 0)
     far_first(lambda j: wpart_copy(j).start())
 
     def take_idx(j):
@@ -224,7 +241,8 @@
         return dot(tiles[owner, s], grads[h][rows[s, owner]], 0, 0)
 
     for h in range(HALVES):
-        each(n_rep, lambda k, h=h: grad_copy(h, k).wait_recv())
+        for t in range(STRIPS):
+            each(n_rep, lambda k, h=h, t=t: grad_copy(h, k, t).wait_recv())
 
         def give(j, h=h):
             owner = blk_to(j)
@@ -263,7 +281,7 @@
         each(n_blk, collect)
         qsend[h] = facc[h].astype(BF16)
         each(n_rep, lambda k, h=h: fpart_copy(h, k).start())
-        if h == 0:
+        if h == HALVES - 1:
             each(n_rep, lambda k: wrep_copy(k).wait_recv())
             wtotal = wrep[0].astype(F32)
             for k in range(1, n_rep):
@@ -289,8 +307,9 @@
     def finish_rep(k):
         wrep_copy(k).wait_send()
         for h in range(HALVES):
-            part_copy(h, k).wait_send()
-            grad_copy(h, k).wait_send()
+            for t in range(STRIPS):
+                part_copy(h, k, t).wait_send()
+                grad_copy(h, k, t).wait_send()
             fpart_copy(h, k).wait_send()
 
     for h in range(HALVES):
@@ -320,6 +339,7 @@
     whole = pl.BlockSpec(memory_space=pl.ANY)
     dma = pltpu.SemaphoreType.DMA
     by_blk, by_rep = dma((HALVES, n_blk)), dma((HALVES, n_rep))
+    by_strip = dma((HALVES, n_rep, STRIPS))
     results = pl.pallas_call(
         functools.partial(layer_kernel, n_blk, n_rep),
         out_shape=(
@@ -342,6 +362,7 @@
             pltpu.VMEM((HALVES, nodes, width), BF16),
             pltpu.VMEM((HALVES, n_rep, chunk, width), BF16),
             pltpu.VMEM((chunk, hidden), BF16),
+            pltpu.VMEM((chunk, hidden), BF16),
             pltpu.VMEM((nodes // tile, tile, width), BF16),
             pltpu.VMEM((nodes // tile, tile, width), BF16),
             pltpu.VMEM((HALVES, n_blk, slots, tile, width), BF16),
@@ -353,7 +374,7 @@
             pltpu.VMEM((n_blk, wchunk, hidden), F32),
             pltpu.VMEM((n_rep, wchunk, hidden), BF16),
             dma((n_blk,)), dma((n_blk,)), dma((n_blk,)),
-            by_blk, by_blk, by_rep, by_rep, by_rep, by_rep,
+            by_blk, by_blk, by_strip, by_strip, by_strip, by_strip,
             by_blk, by_blk, by_rep, by_rep,
             dma((n_blk,)), dma((n_blk,)), dma((n_rep,)), dma((n_rep,)), dma((n_blk,)), dma((n_blk,)),
         ],

time: 59.8 us -> 59 us (0.987)
  Pallas kernels: 58.9 us -> 58.2 us
    pallas_call x1, Pallas kernels: 57 us -> 56.3 us  [on_device(): pl.pallas_call(functools.partial(layer_kernel, n_blk, n_rep), out_shape=(...]
where the time goes in v4:
time: 59 us; the launch traced here: 58.8 us
  Pallas kernels  58.2 us (99%)
  between operations  0.64 us (1%)
    pallas_call x1, Pallas kernels, on_device(): pl.pallas_call(functools.partial(layer_kernel, n_blk, n_rep), out_shape=(...  56.3 us
    pallas_call x1, Pallas kernels, on_device(): pl.pallas_call(hand_over, out_shape=tuple((jax.ShapeDtypeStruct(r.shape,...  1.88 us

profile of v4, /device:TPU:1, one launch (start us, length us, event | category | flops | bytes accessed | tf_op | source)
XLA Modules:
  0.0 58.8 jit_solution(9778690380167406102)
XLA Ops:
  0.6 56.3 %shard_map.94 = (bf16[256,256]{1,0:T(8,128)(2,1)}, bf16[256,256]{1,0:T(8,128)(2,1)}, f32[256,256]{1,0:T(8,128)}) custom-call(bf16[4,256,256]{2,1,0:T(8,128)(2,1)} %bitcast.9, bf16[256,256]{1,0:T(8,128)(2,1)} %weight_in.1, bf16[256,256]{1,0:T(8,128)(2,1)} %cot_in.1, bf16[4,2,256,256]{3,2,1,0:T(8,128)(2,1)} %bitcast.8, s32[2,4]{1,0:T(2,128)} %bitcast.12, ...), custom_call_target="tpu_custom_call" | custom-call | tf_op jit(solution)/shard_map/pallas_call | solution.py:343
  56.9 1.9 %shard_map.95 = (bf16[256,256]{1,0:T(8,128)(2,1)}, bf16[256,256]{1,0:T(8,128)(2,1)}, f32[256,256]{1,0:T(8,128)}) custom-call(bf16[256,256]{1,0:T(8,128)(2,1)} %get-tuple-element.6.out_in, bf16[256,256]{1,0:T(8,128)(2,1)} %get-tuple-element.7.fgrad_in, f32[256,256]{1,0:T(8,128)} %get-tuple-element.8.wgrad_in), custom_call_target="tpu_custom_call" | custom-call | tf_op jit(solution)/shard_map/pallas_call | solution.py:388
